TPU v7x, 32 devices: a whole 2x2x4 slice. The times are simulated.
32 devices in a mesh: dp: 8 (over z, y), blk: 4 (over x, core).
Axes of the slice: x: 2, y: 2, z: 4, core: 2. Of those that a mesh axis runs over, the one named last changes fastest.
Arguments:
- features: bfloat16 [4096, 440], P('dp'), may hold values from -6 to 6
- residual: float32 [4096, 147], P(('dp', 'blk')), may hold values from -6 to 6
- block_weights: float32 [2, 2048, 147], P(None, ('dp', 'blk')), may hold values from -6 to 6
- block_inverse: float32 [2, 2048, 2048], P(None, None, ('dp', 'blk')), as said below
- block_columns: int32 [2, 2048], replicated, may hold values from 0 to 4095, as said below
Outputs:
- residual_out: float32 [4096, 147], P(('dp', 'blk'))
- weights_out: float32 [2, 2048, 147], P(None, ('dp', 'blk'))
Inputs may be any that keep to these rules, and one draw needn't show every extreme that they name: `block_columns`: every frame number appears at most once over both blocks. `block_inverse`: each block's matrix is symmetric and positive definite.
All inputs are finite; a program needn't handle non-finite values.
Results may differ from a plain program's by a relative error of at most 0.011.
Values may be sent and summed in bfloat16 or wider, within the bound.
A program may use at most 64 MiB of HBM per device.

v0:
```python
import jax
import jax.numpy as jnp
from jax import lax
from jax.sharding import PartitionSpec as P

RIDGE = 0.3


def on_device(features, residual, block_weights, block_inverse, block_columns):
    data_count = lax.axis_size("dp")
    block_count = lax.axis_size("blk")
    data_index = lax.axis_index("dp")
    block_index = lax.axis_index("blk")
    row_count, width = features.shape
    own_count = block_weights.shape[1]
    column_count = block_columns.shape[1]
    piece_count = data_count * own_count
    gamma_rate = 4.0 / width
    frame_f = features.astype(jnp.float32)
    frame_sq = jnp.sum(frame_f * frame_f, axis=1)
    current = residual
    results = []
    for section in range(block_columns.shape[0]):
        layout = block_columns[section].reshape(data_count, block_count, own_count)
        chosen = lax.dynamic_index_in_dim(layout, block_index, 1, keepdims=False).reshape(
            piece_count
        )
        local_rows = chosen - data_index * row_count
        inside = (local_rows >= 0) & (local_rows < row_count)
        picked = jnp.take(features, jnp.clip(local_rows, 0, row_count - 1), axis=0).astype(
            jnp.float32
        )
        contrib = jnp.where(inside[:, None], picked, jnp.zeros_like(picked))
        centers = lax.psum(contrib, "dp")
        center_sq = jnp.sum(centers * centers, axis=1)
        cross = lax.dot_general(
            features,
            centers.astype(jnp.bfloat16),
            (((1,), (1,)), ((), ())),
            preferred_element_type=jnp.float32,
        )
        kernel = jnp.exp(
            -gamma_rate * (frame_sq[:, None] + center_sq[None, :] - 2.0 * cross)
        ).astype(jnp.bfloat16)
        partial_value = lax.dot_general(
            kernel,
            lax.all_gather(current.astype(jnp.bfloat16), "blk", axis=0, tiled=True),
            (((0,), (0,)), ((), ())),
            preferred_element_type=jnp.float32,
        )
        weights_own = block_weights[section]
        own_part = (
            lax.dynamic_slice_in_dim(partial_value, data_index * own_count, own_count, 0)
            - RIDGE * weights_own
        )
        partial_value = lax.dynamic_update_slice_in_dim(
            partial_value, own_part, data_index * own_count, 0
        )
        grad_piece = lax.psum(partial_value, "dp")
        stacked = lax.all_gather(grad_piece.astype(jnp.bfloat16), "blk", axis=0, tiled=True).astype(
            grad_piece.dtype
        )
        inverse = block_inverse[section].reshape(data_count, block_count, own_count, own_count)
        inverse = jnp.transpose(inverse, (1, 0, 2, 3)).reshape(column_count, own_count)
        change = lax.dot_general(
            inverse,
            stacked,
            (((0,), (0,)), ((), ())),
            precision=lax.Precision.HIGHEST,
            preferred_element_type=jnp.float32,
        )
        results.append(weights_own + change)
        change_all = lax.all_gather(change.astype(jnp.bfloat16), "dp", axis=0, tiled=True)
        current = current - lax.psum_scatter(
            jnp.dot(kernel, change_all, preferred_element_type=jnp.float32).astype(jnp.bfloat16),
            "blk",
            scatter_dimension=0,
            tiled=True,
        ).astype(jnp.float32)
    return (current, jnp.stack(results))


def solution(mesh):
    placed = (
        P("dp", None),
        P(("dp", "blk"), None),
        P(None, ("dp", "blk"), None),
        P(None, None, ("dp", "blk")),
        P(),
    )
    return jax.shard_map(
        on_device,
        mesh=mesh,
        in_specs=placed,
        out_specs=(P(("dp", "blk"), None), P(None, ("dp", "blk"), None)),
        check_vma=False,
    )
```

profile of v0, /device:TPU:1, one launch (start us, length us, event | category | flops | bytes accessed | tf_op | source)
XLA Modules:
  0.0 335.0 jit_solution(324146737951254708)
XLA Ops:
  7.2 0.8 slice_reduce_fusion.1
  8.5 1.2 copy.39
  9.8 2.0 gather_fusion.1
  11.8 2.0 gather_fusion
  13.8 1.2 convert_select_fusion
  15.0 1.2 convert_select_fusion.1
  16.3 0.8 copy-done.4
  19.8 6.5 %all_gather.18 = bf16[512,147]{0,1:T(8,128)(2,1)S(1)} all-gather(bf16[128,147]{0,1:T(8,128)(2,1)S(1)} %convert_element_type.57), channel_id=1, replica_groups=mesh['dp'=8,'blk'=4] {'blk'}, dimensions={0}, use_global_device_ids=true | all-gather | bytes 188160 | tf_op jit(solution)/shard_map/all_gather | solution.py:47
  26.5 93.9 %all-reduce.5.cloned.1.call-done = (f32[512,440]{1,0:T(8,128)}, f32[512,440]{1,0:T(8,128)}) async-done(((f32[512,440]{1,0:T(8,128)}, f32[512,440]{1,0:T(8,128)}), (f32[512,440]{1,0:T(8,128)}, f32[512,440]{1,0:T(8,128)})) %all-reduce.5.cloned.1.call-update) | async-done | bytes 1802256 | tf_op jit(solution)/shard_map/psum | solution.py:34
  120.4 1.5 multiply_reduce_fusion.1
  123.8 0.8 dynamic_update_slice.6
  124.6 32.6 %all-reduce.6 = bf16[512,147]{0,1:T(8,128)(2,1)S(1)} all-reduce(f32[512,147]{0,1:T(8,128)S(1)} %dynamic_update_slice.6), channel_id=1, replica_groups=mesh['dp'=8,'blk'=4] {'dp'}, use_global_device_ids=true, to_apply=%region_3.5 | all-reduce | flops 75264 | bytes 451584 | tf_op jit(solution)/shard_map/psum | solution.py:59
  157.2 15.3 %all_gather.19 = bf16[2048,147]{0,1:T(8,128)(2,1)S(1)} all-gather(bf16[512,147]{0,1:T(8,128)(2,1)S(1)} %all-reduce.6), channel_id=1, replica_groups=mesh['dp'=8,'blk'=4] {'blk'}, dimensions={0}, use_global_device_ids=true | all-gather | bytes 752640 | tf_op jit(solution)/shard_map/all_gather | solution.py:60
  173.2 24.5 %all_gather.20 = bf16[512,147]{1,0:T(8,128)(2,1)S(1)} all-gather(bf16[64,147]{1,0:T(8,128)(2,1)S(1)} %get-tuple-element.18), channel_id=1, replica_groups=mesh['dp'=8,'blk'=4] {'dp'}, dimensions={0}, use_global_device_ids=true | all-gather | bytes 169344 | tf_op jit(solution)/shard_map/all_gather | solution.py:73
  198.0 0.9 copy.48
  199.6 21.6 %reduce-scatter.7.cloned.1.call-done = bf16[128,147]{1,0:T(8,128)(2,1)} async-done(((bf16[512,147]{1,0:T(8,128)(2,1)}), bf16[128,147]{1,0:T(8,128)(2,1)}) %reduce-scatter.7.cloned.1.call-update) | async-done | bytes 37648
  221.2 0.9 copy.49
  222.2 6.1 %all_gather.21 = bf16[512,147]{0,1:T(8,128)(2,1)S(1)} all-gather(bf16[128,147]{0,1:T(8,128)(2,1)S(1)} %fusion.16), channel_id=1, replica_groups=mesh['dp'=8,'blk'=4] {'blk'}, dimensions={0}, use_global_device_ids=true | all-gather | bytes 188160 | tf_op jit(solution)/shard_map/all_gather | solution.py:47
  229.7 33.9 %all-reduce.7 = bf16[512,147]{0,1:T(8,128)(2,1)S(1)} all-reduce(f32[512,147]{0,1:T(8,128)S(1)} %dynamic_update_slice.7), channel_id=1, replica_groups=mesh['dp'=8,'blk'=4] {'dp'}, use_global_device_ids=true, to_apply=%region_7.9 | all-reduce | flops 75264 | bytes 451584 | tf_op jit(solution)/shard_map/psum | solution.py:59
  263.6 14.0 %all_gather.22 = bf16[2048,147]{0,1:T(8,128)(2,1)S(1)} all-gather(bf16[512,147]{0,1:T(8,128)(2,1)S(1)} %all-reduce.7), channel_id=1, replica_groups=mesh['dp'=8,'blk'=4] {'blk'}, dimensions={0}, use_global_device_ids=true | all-gather | bytes 752640 | tf_op jit(solution)/shard_map/all_gather | solution.py:60
  278.3 24.4 %all_gather.23 = bf16[512,147]{1,0:T(8,128)(2,1)S(1)} all-gather(bf16[64,147]{1,0:T(8,128)(2,1)S(1)} %get-tuple-element.17), channel_id=1, replica_groups=mesh['dp'=8,'blk'=4] {'dp'}, dimensions={0}, use_global_device_ids=true | all-gather | bytes 169344 | tf_op jit(solution)/shard_map/all_gather | solution.py:73
  303.0 0.8 copy.50
  304.5 22.4 %reduce-scatter.9.cloned.1.call-done = bf16[128,147]{1,0:T(8,128)(2,1)} async-done(((bf16[512,147]{1,0:T(8,128)(2,1)}), bf16[128,147]{1,0:T(8,128)(2,1)}) %reduce-scatter.9.cloned.1.call-update) | async-done | bytes 37648
  326.9 0.9 copy.51
  (64 shorter events, 10.9 us)
Async XLA Ops:
  7.2 113.2 %all-reduce.5.cloned.1.call-start = ((), (), s32[]{:S(2)}) async-start(), calls=%async_computation.4 | async-start | bytes 4194304 | tf_op jit(solution)/shard_map/psum | solution.py:34
  16.2 0.9 copy-start.4
  16.2 1.3 copy-start.1
  16.2 205.0 %reduce-scatter.7.cloned.1.call-start = ((), (), s32[]{:S(2)}) async-start(), calls=%async_computation.2 | async-start | bytes 327680
  19.5 6.9 %copy-start = (bf16[512,440]{0,1:T(8,128)(2,1)S(1)}, bf16[512,440]{0,1:T(8,128)(2,1)}, u32[]{:S(2)}) copy-start(bf16[512,440]{0,1:T(8,128)(2,1)} %param.7) | copy-start | bytes 1351684
  120.4 1.5 copy-start.3
  122.8 0.9 copy-start.5
  173.2 25.7 %copy-start.2 = (f32[512,440]{1,0:T(8,128)S(1)}, f32[512,440]{1,0:T(8,128)}, u32[]{:S(2)}) copy-start(f32[512,440]{1,0:T(8,128)} %get-tuple-element.11) | copy-start | bytes 2703364
  198.9 128.0 %reduce-scatter.9.cloned.1.call-start = ((), (), s32[]{:S(2)}) async-start(), calls=%async_computation.3 | async-start | bytes 327680
Sparse Core Ops, SparseCore 0:
  16.4 103.9 all-reduce.4
  199.0 22.1 reduce-scatter.6
  304.0 22.8 reduce-scatter.8
where the time goes:
time: 336 us; the launch traced here: 335 us
  blocking collectives  157 us (47%)
  waiting for transfers between devices  138 us (41%)
  local copies, waits for them, and re-layouts  16.4 us (5%)
  between operations  14 us (4%)
  other arithmetic  5.57 us (2%)
  matrix products  3.73 us (1%)
    psum x1, waiting for transfers between devices, on_device(): centers = lax.psum(contrib, 'dp')  93.9 us
    psum x2, blocking collectives, on_device(): grad_piece = lax.psum(partial_value, 'dp')  66.6 us
    all_gather x2, blocking collectives, on_device(): lax.all_gather(change.astype(jnp.bfloat16), 'dp', axis=0, tiled=True)  48.9 us
    unnamed x5, waiting for transfers between devices  44 us
    all_gather x2, blocking collectives, on_device(): lax.all_gather(grad_piece.astype(jnp.bfloat16), 'blk', axis=0, tiled=True)  29.2 us
    all_gather x2, blocking collectives, on_device(): lax.all_gather(current.astype(jnp.bfloat16), 'blk', axis=0, tiled=True)  12.6 us
    unnamed x19, local copies, waits for them, and re-layouts  6.95 us
  transfers between devices with their start and end apart: 3, of which 3 were waited for; matrix products, arithmetic and copies ran while one was open for 1% of the time, Pallas kernels for 0%

commit v1 on v0

--- a/solution.py
+++ b/solution.py
@@ -1,12 +1,300 @@
+import functools
+
 import jax
 import jax.numpy as jnp
 from jax import lax
+from jax.experimental import pallas as pl
+from jax.experimental.pallas import tpu as pltpu
 from jax.sharding import PartitionSpec as P
 
 RIDGE = 0.3
+MESH = pl.DeviceIdType.MESH
+F32 = jnp.float32
+BF16 = jnp.bfloat16
+FEAT, CUR0, GRAD0, CHANGE0, CUR1, GRAD1, CHANGE1 = range(7)
+DIRECT, ACROSS, BESIDE, LAST = range(4)
+
+
+def nt_dot(a, b):
+    return lax.dot_general(a, b, (((1,), (1,)), ((), ())), preferred_element_type=F32)
+
+
+def nn_dot(a, b):
+    return jnp.dot(a, b, preferred_element_type=F32)
+
+
+def fused_kernel(
+    n,
+    feat_ref,
+    res_ref,
+    weights_ref,
+    inv_ref,
+    own_ref,
+    cols_ref,
+    res_out,
+    weights_out,
+    feat_all,
+    cur_all,
+    grad_all,
+    change_all,
+    inv_parts,
+    kern,
+    kcol,
+    send_sem,
+    recv_sem,
+):
+    d, b = lax.axis_index("dp"), lax.axis_index("blk")
+    groups = 4
+    side = b + 1 - 2 * (b % 2)
+    across = (b + 2) % 4
+    beyond = (side + 2) % 4
+    shard, width = feat_ref.shape
+    rows = shard // groups
+    own = weights_ref.shape[1]
+    cols = cols_ref.shape[1]
+    total = n * shard
+    rate = 4.0 / width
+    buffers = {
+        FEAT: (feat_all, rows),
+        CUR0: (cur_all.at[0], rows),
+        CUR1: (cur_all.at[1], rows),
+        GRAD0: (grad_all.at[0], own),
+        GRAD1: (grad_all.at[1], own),
+        CHANGE0: (change_all.at[0], own),
+        CHANGE1: (change_all.at[1], own),
+    }
+
+    def block(which, source_d, source_b):
+        buf, size = buffers[which]
+        return buf.at[pl.ds(pl.multiple_of((source_d * groups + source_b) * size, size), size)]
+
+    def remote(which, stage, ref, send_k, recv_k, to_d, to_b):
+        return pltpu.make_async_remote_copy(
+            src_ref=ref,
+            dst_ref=ref,
+            send_sem=send_sem.at[which, stage, send_k],
+            recv_sem=recv_sem.at[which, stage, recv_k],
+            device_id={"dp": to_d, "blk": to_b},
+            device_id_type=MESH,
+        )
+
+    def direct(which, k):
+        return remote(which, DIRECT, block(which, d, b), k, n - k, (d + k) % n, b)
+
+    def arrival(which, stage, k):
+        source = {DIRECT: b, ACROSS: across, BESIDE: side, LAST: beyond}[stage]
+        return remote(which, stage, block(which, (d + k) % n, source), k, k, d, side)
+
+    def pass_across(which, k):
+        return remote(which, ACROSS, block(which, (d + k) % n, b), k, k, d, across)
+
+    def pass_beside(which, k):
+        return remote(which, BESIDE, block(which, (d + k) % n, b), k, k, d, side)
+
+    def pass_last(which, k):
+        return remote(which, LAST, block(which, (d + k) % n, across), k, k, d, side)
+
+    def loop(first, last, body):
+        lax.fori_loop(first, last, lambda k, c: (body(k), c)[1], 0)
+
+    def begin(which):
+        loop(1, n, lambda k: direct(which, k).start())
+        if which != FEAT:
+            pass_across(which, 0).start()
+            pass_beside(which, 0).start()
+
+    def forward(which):
+        def step(k):
+            arrival(which, DIRECT, k).wait_recv()
+            pass_across(which, k).start()
+            pass_beside(which, k).start()
+
+        loop(1, n, step)
+
+    def forward_last(which):
+        def step(k):
+            arrival(which, ACROSS, k).wait_recv()
+            pass_last(which, k).start()
+
+        loop(1 if which == FEAT else 0, n, step)
+
+    def finish(which):
+        def step(k):
+            arrival(which, BESIDE, k).wait_recv()
+            arrival(which, LAST, k).wait_recv()
+
+        loop(1 if which == FEAT else 0, n, step)
+
+    def drain(which):
+        loop(1, n, lambda k: direct(which, k).wait_send())
+
+        def step(k):
+            pass_across(which, k).wait_send()
+            pass_beside(which, k).wait_send()
+            pass_last(which, k).wait_send()
+
+        loop(1 if which == FEAT else 0, n, step)
+
+    def own_rows(size):
+        return pl.ds(pl.multiple_of((d * groups + b) * size, size), size)
+
+    mine = pl.ds(pl.multiple_of(b * rows, rows), rows)
+    feat_all[pl.ds(pl.multiple_of(d * shard, shard), shard), :] = feat_ref[...]
+    cur_all[0, own_rows(rows), :] = res_ref[...].astype(BF16)
+
+    barrier = pltpu.get_barrier_semaphore()
+    for k in range(1, n):
+        pl.semaphore_signal(
+            barrier, inc=1, device_id={"dp": (d + k) % n, "blk": b}, device_id_type=MESH
+        )
+    for peer in (side, across):
+        pl.semaphore_signal(barrier, inc=1, device_id={"dp": d, "blk": peer}, device_id_type=MESH)
+    pl.semaphore_wait(barrier, n + 1)
+
+    begin(FEAT)
+    begin(CUR0)
+
+    both = jnp.concatenate([inv_ref[0], inv_ref[1]], axis=1).T
+    high = both.astype(BF16)
+    rest = both - high.astype(F32)
+    middle = rest.astype(BF16)
+    low = (rest - middle.astype(F32)).astype(BF16)
+    for s in range(2):
+        part = slice(s * own, (s + 1) * own)
+        inv_parts[s] = jnp.concatenate([high[part], middle[part], low[part]], axis=0)
+
+    forward(FEAT)
+    forward(CUR0)
+    forward_last(FEAT)
+    forward_last(CUR0)
+    finish(FEAT)
+
+    def pick(c, acc):
+        frames = lax.broadcasted_iota(jnp.int32, (2 * own, shard), 1) + c * shard
+        hot = jnp.where(frames == own_ref[...], 1.0, 0.0).astype(BF16)
+        at = pl.ds(pl.multiple_of(c * shard, shard), shard)
+        return acc + nn_dot(hot, feat_all[at, :])
+
+    centers = lax.fori_loop(0, n, pick, jnp.zeros((2 * own, width), F32))
+    left_f = jnp.concatenate([centers, feat_ref[mine, :].astype(F32)], axis=0)
+    left = left_f.astype(BF16)
+    left_sq = jnp.sum(left_f * left_f, axis=1, keepdims=True)
+    ones = jnp.ones((16, width), BF16)
+
+    def fill(c):
+        at = pl.ds(pl.multiple_of(c * shard, shard), shard)
+        right = feat_all[at, :]
+        right_f = right.astype(F32)
+        square = right_f * right_f
+        square_high = square.astype(BF16)
+        square_low = (square - square_high.astype(F32)).astype(BF16)
+        right_sq = (nt_dot(ones, square_high) + nt_dot(ones, square_low))[0:1, :]
+        cross = nt_dot(left, right)
+        kern[:, at] = jnp.exp(-rate * (left_sq + right_sq - 2.0 * cross)).astype(BF16)
+
+    loop(0, n, fill)
+
+    def spread(s):
+        tile = 512
+
+        def step(c):
+            at = pl.ds(pl.multiple_of(c * tile, tile), tile)
+            wanted = cols_ref[pl.ds(s, 1), at]
+
+            def inner(f, acc):
+                frames = lax.broadcasted_iota(jnp.int32, (shard, tile), 0) + f * shard
+                hot = jnp.where(frames == wanted, 1.0, 0.0).astype(BF16)
+                here = pl.ds(pl.multiple_of(f * shard, shard), shard)
+                return acc + nn_dot(kern[2 * own : 2 * own + rows, here], hot)
+
+            kcol[s, :, at] = lax.fori_loop(0, n, inner, jnp.zeros((rows, tile), F32)).astype(BF16)
+
+        loop(0, cols // tile, step)
+
+    current = res_ref[...]
+    finish(CUR0)
+    for s, cur, grad, change in ((0, CUR0, GRAD0, CHANGE0), (1, CUR1, GRAD1, CHANGE1)):
+        gradient = nn_dot(kern[s * own : (s + 1) * own, :], cur_all[s]) - RIDGE * weights_ref[s]
+        grad_all[s, own_rows(own), :] = gradient.astype(BF16)
+        begin(grad)
+        if s == 0:
+            spread(0)
+        forward(grad)
+        forward_last(grad)
+        finish(grad)
+        parts = nn_dot(inv_parts[s], grad_all[s])
+        delta = parts[0:own] + (parts[own : 2 * own] + parts[2 * own : 3 * own])
+        change_all[s, own_rows(own), :] = delta.astype(BF16)
+        begin(change)
+        weights_out[s] = weights_ref[s] + delta
+        if s == 0:
+            spread(1)
+        forward(change)
+        forward_last(change)
+        finish(change)
+        current = current - nn_dot(kcol[s], change_all[s])
+        if s == 0:
+            cur_all[1, own_rows(rows), :] = current.astype(BF16)
+            begin(CUR1)
+            forward(CUR1)
+            forward_last(CUR1)
+            finish(CUR1)
+    res_out[...] = current
+    for which in range(7):
+        drain(which)
+
+
+def fused(features, residual, block_weights, block_inverse, block_columns):
+    n = lax.axis_size("dp")
+    groups = lax.axis_size("blk")
+    shard, width = features.shape
+    rows, classes = residual.shape
+    own = block_weights.shape[1]
+    cols = block_columns.shape[1]
+    place = lax.axis_index("dp") * groups + lax.axis_index("blk")
+    own_columns = lax.dynamic_slice_in_dim(block_columns, place * own, own, 1).reshape(2 * own, 1)
+    vmem = pl.BlockSpec(memory_space=pltpu.VMEM)
+    return pl.pallas_call(
+        functools.partial(fused_kernel, n),
+        out_shape=(
+            jax.ShapeDtypeStruct(residual.shape, F32),
+            jax.ShapeDtypeStruct(block_weights.shape, F32),
+        ),
+        in_specs=[vmem] * 6,
+        out_specs=(vmem, vmem),
+        scratch_shapes=[
+            pltpu.VMEM((n * shard, width), BF16),
+            pltpu.VMEM((2, n * shard, classes), BF16),
+            pltpu.VMEM((2, cols, classes), BF16),
+            pltpu.VMEM((2, cols, classes), BF16),
+            pltpu.VMEM((2, 3 * own, cols), BF16),
+            pltpu.VMEM((2 * own + rows, n * shard), BF16),
+            pltpu.VMEM((2, rows, cols), BF16),
+            pltpu.SemaphoreType.DMA((7, 4, n)),
+            pltpu.SemaphoreType.DMA((7, 4, n)),
+        ],
+        compiler_params=pltpu.CompilerParams(
+            collective_id=0, has_side_effects=True, vmem_limit_bytes=48 * 2**20
+        ),
+    )(features, residual, block_weights, block_inverse, own_columns, block_columns)
+
+
+def fits(features, residual, block_weights, block_columns):
+    n, groups = lax.axis_size("dp"), lax.axis_size("blk")
+    shard, width = features.shape
+    own = block_weights.shape[1]
+    return (
+        groups == 4
+        and block_columns.shape[0] == 2
+        and own == 64
+        and residual.shape[0] == 128
+        and n * shard * (width + 512) <= 6 * 2**20
+    )
 
 
 def on_device(features, residual, block_weights, block_inverse, block_columns):
+    if fits(features, residual, block_weights, block_columns):
+        return fused(features, residual, block_weights, block_inverse, block_columns)
     data_count = lax.axis_size("dp")
     block_count = lax.axis_size("blk")
     data_index = lax.axis_index("dp")

time: 336 us -> 166 us (0.49)
  blocking collectives: 157 us -> 0 us
  Pallas kernels: 0 us -> 156 us
  waiting for transfers between devices: 138 us -> 0 us
  between operations: 14 us -> 0.71 us
  local copies, waits for them, and re-layouts: 16.4 us -> 6.35 us
  other arithmetic: 5.57 us -> 0 us
  matrix products: 3.73 us -> 0 us
    pallas_call x0 -> x1, Pallas kernels: none -> 156 us  [fused(): pl.pallas_call(functools.partial(fused_kernel, n), out_shape=(jax.ShapeDt...]
    psum x1 -> x0, waiting for transfers between devices: 93.9 us -> none  [on_device(): centers = lax.psum(contrib, 'dp')]
    all_gather x6 -> x0, blocking collectives: 90.7 us -> none  [the longest x2 48.9 us: on_device(): lax.all_gather(change.astype(jnp.bfloat16), 'dp', axis=0, tiled=True)]
    psum x2 -> x0, blocking collectives: 66.6 us -> none  [on_device(): grad_piece = lax.psum(partial_value, 'dp')]
    unnamed x5 -> x0, waiting for transfers between devices: 44 us -> none
    gather x2 -> x0, local copies, waits for them, and re-layouts: 3.94 us -> none  [on_device(): jnp.take(features, jnp.clip(local_rows, 0, row_count - 1), axis=0)]
    dot_general x8 -> x0, matrix products: 3.73 us -> none  [the longest x2 1.47 us: on_device(): lax.dot_general(inverse, stacked, (((0,), (0,)), ((), ())), precision=lax...]
    unnamed x19 -> x8, local copies, waits for them, and re-layouts: 6.95 us -> 4.73 us
  transfers between devices with their start and end apart: 3 -> 0, of which waited for: 3 -> 0; matrix products, arithmetic and copies ran while one was open for 1% -> 0% of each run, Pallas kernels for 0% -> 0%
where the time goes in v1:
time: 166 us; the launch traced here: 163 us
  Pallas kernels  156 us (94%)
  local copies, waits for them, and re-layouts  6.35 us (4%)
    pallas_call x1, Pallas kernels, fused(): pl.pallas_call(functools.partial(fused_kernel, n), out_shape=(jax.ShapeDt...  156 us
    unnamed x8, local copies, waits for them, and re-layouts  4.73 us

profile of v1, /device:TPU:1, one launch (start us, length us, event | category | flops | bytes accessed | tf_op | source)
XLA Modules:
  0.0 162.9 jit_solution(7981367025543250810)
XLA Ops:
  0.6 0.8 constant_dynamic-slice_fusion
  1.4 0.1 reshape.8.own_ref
  1.5 1.0 copy.8.res_ref
  2.5 0.0 copy-start
  2.5 0.0 copy-start.1
  2.5 1.3 copy.7.feat_ref
  3.8 1.8 %copy.9.inv_ref = f32[2,2048,64]{2,1,0:T(8,128)S(1)} copy(f32[2,2048,64]{1,2,0:T(8,128)} %param.8) | data formatting | bytes 2097152 | tf_op args[3]
  5.6 0.0 copy-done
  5.6 0.0 copy-done.1
  5.7 155.8 %shard_map.68 = (f32[128,147]{1,0:T(8,128)S(1)}, f32[2,64,147]{2,1,0:T(8,128)S(1)}) custom-call(bf16[512,440]{1,0:T(8,128)(2,1)S(1)} %copy.7.feat_ref, f32[128,147]{1,0:T(8,128)S(1)} %copy.8.res_ref, f32[2,64,147]{2,1,0:T(8,128)S(1)} %copy-done, f32[2,2048,64]{2,1,0:T(8,128)S(1)} %copy.9.inv_ref, s32[128,1]{1,0:T(8,128)S(1)} %reshape.8.own_ref, ...), custom_call_target="tpu_custom_call" | custom-call | tf_op jit(solution)/shard_map/pallas_call | solution.py:257
  161.5 0.7 copy.11
  162.3 0.7 copy.13
Async XLA Ops:
  2.5 3.1 %copy-start = (f32[2,64,147]{2,1,0:T(8,128)S(1)}, f32[2,64,147]{2,1,0:T(8,128)}, u32[]{:S(2)}) copy-start(f32[2,64,147]{2,1,0:T(8,128)} %weights_ref.1) | copy-start | bytes 225796
  2.5 3.1 %copy-start.1 = (s32[2,2048]{1,0:T(2,128)S(1)}, s32[2,2048]{1,0:T(2,128)}, u32[]{:S(2)}) copy-start(s32[2,2048]{1,0:T(2,128)} %cols_ref.1) | copy-start | bytes 49156

commit v2 on v1

--- a/solution.py
+++ b/solution.py
@@ -40,6 +40,8 @@
     inv_parts,
     kern,
     kcol,
+    res_pad,
+    weights_pad,
     send_sem,
     recv_sem,
 ):
@@ -48,25 +50,26 @@
     side = b + 1 - 2 * (b % 2)
     across = (b + 2) % 4
     beyond = (side + 2) % 4
-    shard, width = feat_ref.shape
+    width, shard = feat_ref.shape
+    depth = feat_all.shape[1]
     rows = shard // groups
-    own = weights_ref.shape[1]
+    own, classes = weights_ref.shape[1:]
     cols = cols_ref.shape[1]
     total = n * shard
     rate = 4.0 / width
+    slot = d * groups + b
     buffers = {
-        FEAT: (feat_all, rows),
-        CUR0: (cur_all.at[0], rows),
-        CUR1: (cur_all.at[1], rows),
-        GRAD0: (grad_all.at[0], own),
-        GRAD1: (grad_all.at[1], own),
-        CHANGE0: (change_all.at[0], own),
-        CHANGE1: (change_all.at[1], own),
+        FEAT: feat_all,
+        CUR0: cur_all.at[0],
+        CUR1: cur_all.at[1],
+        GRAD0: grad_all.at[0],
+        GRAD1: grad_all.at[1],
+        CHANGE0: change_all.at[0],
+        CHANGE1: change_all.at[1],
     }
 
     def block(which, source_d, source_b):
-        buf, size = buffers[which]
-        return buf.at[pl.ds(pl.multiple_of((source_d * groups + source_b) * size, size), size)]
+        return buffers[which].at[source_d * groups + source_b]
 
     def remote(which, stage, ref, send_k, recv_k, to_d, to_b):
         return pltpu.make_async_remote_copy(
@@ -135,12 +138,35 @@
 
         loop(1 if which == FEAT else 0, n, step)
 
-    def own_rows(size):
-        return pl.ds(pl.multiple_of((d * groups + b) * size, size), size)
-
-    mine = pl.ds(pl.multiple_of(b * rows, rows), rows)
-    feat_all[pl.ds(pl.multiple_of(d * shard, shard), shard), :] = feat_ref[...]
-    cur_all[0, own_rows(rows), :] = res_ref[...].astype(BF16)
+    def pack(values):
+        count = values.shape[0] // 4
+        lane = lax.broadcasted_iota(jnp.int32, (values.shape[0], 128), 1)
+        tail = jnp.where(lane < classes - 128, values[:, 128:], 0.0)
+        folded = tail[0:count]
+        for q in range(1, 4):
+            folded = folded + pltpu.roll(tail[q * count : (q + 1) * count], 32 * q, 1)
+        return jnp.concatenate([values[:, :128], folded], axis=0).astype(BF16)
+
+    def unpack(packed):
+        slots, size = packed.shape[0], packed.shape[1] * 4 // 5
+        main = packed[:, :size, :].reshape(slots * size, 128)
+        folded = packed[:, size:, :].astype(F32).reshape(slots * size // 4, 128)
+        parts = [folded] + [pltpu.roll(folded, 128 - 32 * q, 1) for q in range(1, 4)]
+        parts = [p.astype(BF16).reshape(slots, size // 4, 128) for p in parts]
+        tail = jnp.concatenate(parts, axis=1).reshape(slots * size, 128)
+        return jnp.concatenate([main, tail], axis=1)
+
+    res_pad[...] = jnp.zeros_like(res_pad)
+    res_pad[0:classes, :] = res_ref[...]
+    weights_pad[...] = jnp.zeros_like(weights_pad)
+    weights_pad[:, :, 0:classes] = weights_ref[...]
+    current = res_pad[...].T
+    filled = jnp.concatenate(
+        [feat_ref[...].astype(F32), jnp.zeros((depth - width, shard), F32)], axis=0
+    ).astype(BF16)
+    for q in range(groups):
+        feat_all[d * groups + q] = filled[:, q * rows : (q + 1) * rows]
+    cur_all[0, slot] = pack(current)
 
     barrier = pltpu.get_barrier_semaphore()
     for k in range(1, n):
@@ -154,7 +180,7 @@
     begin(FEAT)
     begin(CUR0)
 
-    both = jnp.concatenate([inv_ref[0], inv_ref[1]], axis=1).T
+    both = inv_ref[...].reshape(2 * own, cols)
     high = both.astype(BF16)
     rest = both - high.astype(F32)
     middle = rest.astype(BF16)
@@ -163,83 +189,96 @@
         part = slice(s * own, (s + 1) * own)
         inv_parts[s] = jnp.concatenate([high[part], middle[part], low[part]], axis=0)
 
-    forward(FEAT)
-    forward(CUR0)
-    forward_last(FEAT)
-    forward_last(CUR0)
+    def first_forward(k):
+        for which in (FEAT, CUR0):
+            arrival(which, DIRECT, k).wait_recv()
+            pass_across(which, k).start()
+            pass_beside(which, k).start()
+
+    def first_last(k):
+        for which in (FEAT, CUR0):
+            arrival(which, ACROSS, k).wait_recv()
+            pass_last(which, k).start()
+
+    loop(1, n, first_forward)
+    arrival(CUR0, ACROSS, 0).wait_recv()
+    pass_last(CUR0, 0).start()
+    loop(1, n, first_last)
     finish(FEAT)
 
+    row = lax.broadcasted_iota(jnp.int32, (rows, rows), 0)
+    lane = lax.broadcasted_iota(jnp.int32, (rows, rows), 1)
+    same = jnp.where(row == lane, 1.0, 0.0).astype(BF16)
+    frames_own = nt_dot(same, feat_all[slot])
+
     def pick(c, acc):
-        frames = lax.broadcasted_iota(jnp.int32, (2 * own, shard), 1) + c * shard
-        hot = jnp.where(frames == own_ref[...], 1.0, 0.0).astype(BF16)
-        at = pl.ds(pl.multiple_of(c * shard, shard), shard)
-        return acc + nn_dot(hot, feat_all[at, :])
-
-    centers = lax.fori_loop(0, n, pick, jnp.zeros((2 * own, width), F32))
-    left_f = jnp.concatenate([centers, feat_ref[mine, :].astype(F32)], axis=0)
+        for q in range(groups):
+            frames = lax.broadcasted_iota(jnp.int32, (2 * own, rows), 1) + (c * groups + q) * rows
+            hot = jnp.where(frames == own_ref[...], 1.0, 0.0).astype(BF16)
+            acc = acc + nt_dot(hot, feat_all[c * groups + q])
+        return acc
+
+    centers = lax.fori_loop(0, n, pick, jnp.zeros((2 * own, depth), F32))
+    left_f = jnp.concatenate([centers, frames_own], axis=0)
     left = left_f.astype(BF16)
     left_sq = jnp.sum(left_f * left_f, axis=1, keepdims=True)
-    ones = jnp.ones((16, width), BF16)
 
     def fill(c):
         at = pl.ds(pl.multiple_of(c * shard, shard), shard)
-        right = feat_all[at, :]
+        right = jnp.concatenate([feat_all[c * groups + q] for q in range(groups)], axis=1)
         right_f = right.astype(F32)
-        square = right_f * right_f
-        square_high = square.astype(BF16)
-        square_low = (square - square_high.astype(F32)).astype(BF16)
-        right_sq = (nt_dot(ones, square_high) + nt_dot(ones, square_low))[0:1, :]
-        cross = nt_dot(left, right)
+        right_sq = jnp.sum(right_f * right_f, axis=0, keepdims=True)
+        cross = nn_dot(left, right)
         kern[:, at] = jnp.exp(-rate * (left_sq + right_sq - 2.0 * cross)).astype(BF16)
 
     loop(0, n, fill)
 
-    def spread(s):
-        tile = 512
-
-        def step(c):
-            at = pl.ds(pl.multiple_of(c * tile, tile), tile)
-            wanted = cols_ref[pl.ds(s, 1), at]
-
-            def inner(f, acc):
-                frames = lax.broadcasted_iota(jnp.int32, (shard, tile), 0) + f * shard
-                hot = jnp.where(frames == wanted, 1.0, 0.0).astype(BF16)
-                here = pl.ds(pl.multiple_of(f * shard, shard), shard)
-                return acc + nn_dot(kern[2 * own : 2 * own + rows, here], hot)
-
-            kcol[s, :, at] = lax.fori_loop(0, n, inner, jnp.zeros((rows, tile), F32)).astype(BF16)
-
-        loop(0, cols // tile, step)
-
-    current = res_ref[...]
+    tile = cols // 4
+
+    def spread(s, c):
+        at = pl.ds(c * tile, tile)
+        wanted = cols_ref[s : s + 1, at]
+
+        def inner(f, acc):
+            frames = lax.broadcasted_iota(jnp.int32, (shard, tile), 0) + f * shard
+            hot = jnp.where(frames == wanted, 1.0, 0.0).astype(BF16)
+            here = pl.ds(pl.multiple_of(f * shard, shard), shard)
+            return acc + nn_dot(kern[2 * own : 2 * own + rows, here], hot)
+
+        kcol[s, :, at] = lax.fori_loop(0, n, inner, jnp.zeros((rows, tile), F32)).astype(BF16)
+
+    def gather(which, early=None, late=None):
+        begin(which)
+        if early is not None:
+            spread(*early)
+        forward(which)
+        if late is not None:
+            spread(*late)
+        forward_last(which)
+        finish(which)
+
     finish(CUR0)
-    for s, cur, grad, change in ((0, CUR0, GRAD0, CHANGE0), (1, CUR1, GRAD1, CHANGE1)):
-        gradient = nn_dot(kern[s * own : (s + 1) * own, :], cur_all[s]) - RIDGE * weights_ref[s]
-        grad_all[s, own_rows(own), :] = gradient.astype(BF16)
-        begin(grad)
+    for s, grad, change in ((0, GRAD0, CHANGE0), (1, GRAD1, CHANGE1)):
+        gradient = nn_dot(kern[s * own : (s + 1) * own, :], unpack(cur_all[s]))
+        gradient = gradient - RIDGE * weights_pad[s]
+        grad_all[s, slot] = pack(gradient)
         if s == 0:
-            spread(0)
-        forward(grad)
-        forward_last(grad)
-        finish(grad)
-        parts = nn_dot(inv_parts[s], grad_all[s])
+            gather(grad, (0, 0), (0, 1))
+        else:
+            gather(grad, (1, 2), (1, 3))
+        parts = nn_dot(inv_parts[s], unpack(grad_all[s]))
         delta = parts[0:own] + (parts[own : 2 * own] + parts[2 * own : 3 * own])
-        change_all[s, own_rows(own), :] = delta.astype(BF16)
-        begin(change)
-        weights_out[s] = weights_ref[s] + delta
+        change_all[s, slot] = pack(delta)
+        weights_out[s] = weights_ref[s] + delta[:, :classes]
         if s == 0:
-            spread(1)
-        forward(change)
-        forward_last(change)
-        finish(change)
-        current = current - nn_dot(kcol[s], change_all[s])
+            gather(change, (0, 2), (0, 3))
+        else:
+            gather(change)
+        current = current - nn_dot(kcol[s], unpack(change_all[s]))
         if s == 0:
-            cur_all[1, own_rows(rows), :] = current.astype(BF16)
-            begin(CUR1)
-            forward(CUR1)
-            forward_last(CUR1)
-            finish(CUR1)
-    res_out[...] = current
+            cur_all[1, slot] = pack(current)
+            gather(CUR1, (1, 0), (1, 1))
+    res_out[...] = current.T[0:classes, :]
     for which in range(7):
         drain(which)
 
@@ -251,43 +290,57 @@
     rows, classes = residual.shape
     own = block_weights.shape[1]
     cols = block_columns.shape[1]
+    slots = n * groups
+    depth = (width + 15) // 16 * 16
     place = lax.axis_index("dp") * groups + lax.axis_index("blk")
     own_columns = lax.dynamic_slice_in_dim(block_columns, place * own, own, 1).reshape(2 * own, 1)
     vmem = pl.BlockSpec(memory_space=pltpu.VMEM)
-    return pl.pallas_call(
+    res, weights = pl.pallas_call(
         functools.partial(fused_kernel, n),
         out_shape=(
-            jax.ShapeDtypeStruct(residual.shape, F32),
+            jax.ShapeDtypeStruct((classes, rows), F32),
             jax.ShapeDtypeStruct(block_weights.shape, F32),
         ),
         in_specs=[vmem] * 6,
         out_specs=(vmem, vmem),
         scratch_shapes=[
-            pltpu.VMEM((n * shard, width), BF16),
-            pltpu.VMEM((2, n * shard, classes), BF16),
-            pltpu.VMEM((2, cols, classes), BF16),
-            pltpu.VMEM((2, cols, classes), BF16),
+            pltpu.VMEM((slots, depth, rows), BF16),
+            pltpu.VMEM((2, slots, rows + rows // 4, 128), BF16),
+            pltpu.VMEM((2, slots, own + own // 4, 128), BF16),
+            pltpu.VMEM((2, slots, own + own // 4, 128), BF16),
             pltpu.VMEM((2, 3 * own, cols), BF16),
             pltpu.VMEM((2 * own + rows, n * shard), BF16),
             pltpu.VMEM((2, rows, cols), BF16),
+            pltpu.VMEM((256, rows), F32),
+            pltpu.VMEM((2, own, 256), F32),
             pltpu.SemaphoreType.DMA((7, 4, n)),
             pltpu.SemaphoreType.DMA((7, 4, n)),
         ],
         compiler_params=pltpu.CompilerParams(
             collective_id=0, has_side_effects=True, vmem_limit_bytes=48 * 2**20
         ),
-    )(features, residual, block_weights, block_inverse, own_columns, block_columns)
+    )(
+        features.T,
+        residual.T,
+        block_weights,
+        jnp.swapaxes(block_inverse, 1, 2),
+        own_columns,
+        block_columns,
+    )
+    return res.T, weights
 
 
 def fits(features, residual, block_weights, block_columns):
     n, groups = lax.axis_size("dp"), lax.axis_size("blk")
     shard, width = features.shape
-    own = block_weights.shape[1]
+    own, classes = block_weights.shape[1:]
     return (
         groups == 4
         and block_columns.shape[0] == 2
         and own == 64
         and residual.shape[0] == 128
+        and 128 < classes <= 160
+        and width % 8 == 0
         and n * shard * (width + 512) <= 6 * 2**20
     )
 

time: 166 us -> 133 us (0.80); the launches traced: 163 us -> 133 us
  Pallas kernels: 156 us -> 127 us
    pallas_call x1, Pallas kernels: 156 us -> 127 us  [fused(): pl.pallas_call(functools.partial(fused_kernel, n), out_shape=(jax.ShapeDt...]
    unnamed x8 -> x12, local copies, waits for them, and re-layouts: 4.73 us -> 5.13 us
where the time goes in v2:
time: 133 us
  Pallas kernels  127 us (95%)
  local copies, waits for them, and re-layouts  5.34 us (4%)
    pallas_call x1, Pallas kernels, fused(): pl.pallas_call(functools.partial(fused_kernel, n), out_shape=(jax.ShapeDt...  127 us
    unnamed x12, local copies, waits for them, and re-layouts  5.13 us

profile of v2, /device:TPU:1, one launch (start us, length us, event | category | flops | bytes accessed | tf_op | source)
XLA Modules:
  0.0 132.9 jit_solution(2638794122107387615)
XLA Ops:
  0.6 0.0 copy-start.4
  0.6 0.0 copy-start.3
  0.7 0.7 copy-done.4
  1.3 0.1 constant_dynamic-slice_fusion
  1.4 0.1 reshape.8.own_ref
  1.6 0.0 copy-done.3
  1.6 0.0 copy-start
  1.6 1.2 copy-done
  2.8 0.0 copy-start.1
  2.8 1.0 copy-done.1
  3.8 0.0 copy-start.2
  3.8 0.9 copy-done.2
  4.7 126.8 %shard_map.68 = (f32[147,128]{1,0:T(8,128)S(1)}, f32[2,64,147]{2,1,0:T(8,128)S(1)}) custom-call(bf16[440,512]{1,0:T(8,128)(2,1)S(1)} %bitcast.5, f32[147,128]{1,0:T(8,128)S(1)} %bitcast.6, f32[2,64,147]{2,1,0:T(8,128)S(1)} %copy-done.2, f32[2,64,2048]{2,1,0:T(8,128)S(1)} %bitcast.4, s32[128,1]{1,0:T(8,128)S(1)} %reshape.8.own_ref, s32[2,2048]{1,0:T(2,128)S(1)} %copy-done.4), custom_call_target="tpu_custom_call" | custom-call | tf_op jit(solution)/shard_map/pallas_call | solution.py:298
  131.6 0.6 copy.10
  132.2 0.7 copy.11
Async XLA Ops:
  0.6 0.7 copy-start.4
  0.6 0.9 copy-start.3
  1.6 1.2 copy-start
  2.8 1.0 copy-start.1
  3.8 0.9 copy-start.2

commit v3 on v2

--- a/solution.py
+++ b/solution.py
@@ -57,7 +57,9 @@
     cols = cols_ref.shape[1]
     total = n * shard
     rate = 4.0 / width
-    slot = d * groups + b
+    slot = b * n + d
+    half = n // 2
+    near = d // half
     buffers = {
         FEAT: feat_all,
         CUR0: cur_all.at[0],
@@ -69,7 +71,7 @@
     }
 
     def block(which, source_d, source_b):
-        return buffers[which].at[source_d * groups + source_b]
+        return buffers[which].at[source_b * n + source_d]
 
     def remote(which, stage, ref, send_k, recv_k, to_d, to_b):
         return pltpu.make_async_remote_copy(
@@ -100,43 +102,63 @@
     def loop(first, last, body):
         lax.fori_loop(first, last, lambda k, c: (body(k), c)[1], 0)
 
+    def chunk(which, source_b, part):
+        return buffers[which].at[pl.ds(source_b * n + part * half, half)]
+
+    def push(which, to_d):
+        return remote(which, DIRECT, block(which, d, b), to_d, d, to_d, b)
+
+    def landed(which, from_d):
+        return remote(which, DIRECT, block(which, from_d, b), from_d, from_d, d, side)
+
+    def chunk_across(which, part):
+        return remote(which, ACROSS, chunk(which, b, part), part, part, d, across)
+
+    def chunk_beside(which, part):
+        return remote(which, BESIDE, chunk(which, b, part), part, part, d, side)
+
+    def chunk_last(which, part):
+        return remote(which, LAST, chunk(which, across, part), part, part, d, side)
+
+    def chunk_arrival(which, stage, part):
+        source = {ACROSS: across, BESIDE: side, LAST: beyond}[stage]
+        return remote(which, stage, chunk(which, source, part), part, part, d, side)
+
+    def near_peer(k):
+        return near * half + (d + k) % half
+
+    def far_peer(k):
+        return (1 - near) * half + (d + k) % half
+
     def begin(which):
-        loop(1, n, lambda k: direct(which, k).start())
-        if which != FEAT:
-            pass_across(which, 0).start()
-            pass_beside(which, 0).start()
+        loop(1, half, lambda k: push(which, near_peer(k)).start())
+        loop(0, half, lambda k: push(which, far_peer(k)).start())
 
     def forward(which):
-        def step(k):
-            arrival(which, DIRECT, k).wait_recv()
-            pass_across(which, k).start()
-            pass_beside(which, k).start()
-
-        loop(1, n, step)
+        loop(1, half, lambda k: landed(which, near_peer(k)).wait_recv())
+        chunk_across(which, near).start()
+        chunk_beside(which, near).start()
+        loop(0, half, lambda k: landed(which, far_peer(k)).wait_recv())
+        chunk_across(which, 1 - near).start()
+        chunk_beside(which, 1 - near).start()
 
     def forward_last(which):
-        def step(k):
-            arrival(which, ACROSS, k).wait_recv()
-            pass_last(which, k).start()
-
-        loop(1 if which == FEAT else 0, n, step)
+        for part in (near, 1 - near):
+            chunk_arrival(which, ACROSS, part).wait_recv()
+            chunk_last(which, part).start()
 
     def finish(which):
-        def step(k):
-            arrival(which, BESIDE, k).wait_recv()
-            arrival(which, LAST, k).wait_recv()
-
-        loop(1 if which == FEAT else 0, n, step)
+        for stage in (BESIDE, LAST):
+            for part in (near, 1 - near):
+                chunk_arrival(which, stage, part).wait_recv()
 
     def drain(which):
-        loop(1, n, lambda k: direct(which, k).wait_send())
-
-        def step(k):
-            pass_across(which, k).wait_send()
-            pass_beside(which, k).wait_send()
-            pass_last(which, k).wait_send()
-
-        loop(1 if which == FEAT else 0, n, step)
+        loop(1, half, lambda k: push(which, near_peer(k)).wait_send())
+        loop(0, half, lambda k: push(which, far_peer(k)).wait_send())
+        for part in (near, 1 - near):
+            chunk_across(which, part).wait_send()
+            chunk_beside(which, part).wait_send()
+            chunk_last(which, part).wait_send()
 
     def pack(values):
         count = values.shape[0] // 4
@@ -148,6 +170,8 @@
         return jnp.concatenate([values[:, :128], folded], axis=0).astype(BF16)
 
     def unpack(packed):
+        order = [packed[q * n + c][None] for c in range(n) for q in range(groups)]
+        packed = jnp.concatenate(order, axis=0)
         slots, size = packed.shape[0], packed.shape[1] * 4 // 5
         main = packed[:, :size, :].reshape(slots * size, 128)
         folded = packed[:, size:, :].astype(F32).reshape(slots * size // 4, 128)
@@ -165,7 +189,7 @@
         [feat_ref[...].astype(F32), jnp.zeros((depth - width, shard), F32)], axis=0
     ).astype(BF16)
     for q in range(groups):
-        feat_all[d * groups + q] = filled[:, q * rows : (q + 1) * rows]
+        feat_all[q * n + d] = filled[:, q * rows : (q + 1) * rows]
     cur_all[0, slot] = pack(current)
 
     barrier = pltpu.get_barrier_semaphore()
@@ -177,7 +201,7 @@
         pl.semaphore_signal(barrier, inc=1, device_id={"dp": d, "blk": peer}, device_id_type=MESH)
     pl.semaphore_wait(barrier, n + 1)
 
-    begin(FEAT)
+    loop(1, n, lambda k: direct(FEAT, k).start())
     begin(CUR0)
 
     both = inv_ref[...].reshape(2 * own, cols)
@@ -189,22 +213,30 @@
         part = slice(s * own, (s + 1) * own)
         inv_parts[s] = jnp.concatenate([high[part], middle[part], low[part]], axis=0)
 
-    def first_forward(k):
-        for which in (FEAT, CUR0):
-            arrival(which, DIRECT, k).wait_recv()
-            pass_across(which, k).start()
-            pass_beside(which, k).start()
-
-    def first_last(k):
-        for which in (FEAT, CUR0):
-            arrival(which, ACROSS, k).wait_recv()
-            pass_last(which, k).start()
-
-    loop(1, n, first_forward)
-    arrival(CUR0, ACROSS, 0).wait_recv()
-    pass_last(CUR0, 0).start()
-    loop(1, n, first_last)
-    finish(FEAT)
+    def feat_forward(k):
+        arrival(FEAT, DIRECT, k).wait_recv()
+        pass_across(FEAT, k).start()
+        pass_beside(FEAT, k).start()
+
+    def feat_last(k):
+        arrival(FEAT, ACROSS, k).wait_recv()
+        pass_last(FEAT, k).start()
+
+    def feat_finish(k):
+        arrival(FEAT, BESIDE, k).wait_recv()
+        arrival(FEAT, LAST, k).wait_recv()
+
+    def feat_drain(k):
+        direct(FEAT, k).wait_send()
+        pass_across(FEAT, k).wait_send()
+        pass_beside(FEAT, k).wait_send()
+        pass_last(FEAT, k).wait_send()
+
+    loop(1, n, feat_forward)
+    forward(CUR0)
+    loop(1, n, feat_last)
+    forward_last(CUR0)
+    loop(1, n, feat_finish)
 
     row = lax.broadcasted_iota(jnp.int32, (rows, rows), 0)
     lane = lax.broadcasted_iota(jnp.int32, (rows, rows), 1)
@@ -213,9 +245,10 @@
 
     def pick(c, acc):
         for q in range(groups):
-            frames = lax.broadcasted_iota(jnp.int32, (2 * own, rows), 1) + (c * groups + q) * rows
-            hot = jnp.where(frames == own_ref[...], 1.0, 0.0).astype(BF16)
-            acc = acc + nt_dot(hot, feat_all[c * groups + q])
+            frames = lax.broadcasted_iota(jnp.int32, (2 * own, rows), 1)
+            wanted = own_ref[...] - (c * groups + q) * rows
+            hot = jnp.where(frames == wanted, 1.0, 0.0).astype(BF16)
+            acc = acc + nt_dot(hot, feat_all[q * n + c])
         return acc
 
     centers = lax.fori_loop(0, n, pick, jnp.zeros((2 * own, depth), F32))
@@ -225,7 +258,7 @@
 
     def fill(c):
         at = pl.ds(pl.multiple_of(c * shard, shard), shard)
-        right = jnp.concatenate([feat_all[c * groups + q] for q in range(groups)], axis=1)
+        right = jnp.concatenate([feat_all[q * n + c] for q in range(groups)], axis=1)
         right_f = right.astype(F32)
         right_sq = jnp.sum(right_f * right_f, axis=0, keepdims=True)
         cross = nn_dot(left, right)
@@ -240,8 +273,8 @@
         wanted = cols_ref[s : s + 1, at]
 
         def inner(f, acc):
-            frames = lax.broadcasted_iota(jnp.int32, (shard, tile), 0) + f * shard
-            hot = jnp.where(frames == wanted, 1.0, 0.0).astype(BF16)
+            frames = lax.broadcasted_iota(jnp.int32, (shard, tile), 0)
+            hot = jnp.where(frames == wanted - f * shard, 1.0, 0.0).astype(BF16)
             here = pl.ds(pl.multiple_of(f * shard, shard), shard)
             return acc + nn_dot(kern[2 * own : 2 * own + rows, here], hot)
 
@@ -279,7 +312,8 @@
             cur_all[1, slot] = pack(current)
             gather(CUR1, (1, 0), (1, 1))
     res_out[...] = current.T[0:classes, :]
-    for which in range(7):
+    loop(1, n, feat_drain)
+    for which in range(1, 7):
         drain(which)
 
 
@@ -341,6 +375,7 @@
         and residual.shape[0] == 128
         and 128 < classes <= 160
         and width % 8 == 0
+        and n == 8
         and n * shard * (width + 512) <= 6 * 2**20
     )
 

time: 133 us -> 132 us (level)
  Pallas kernels: 127 us -> 125 us
    pallas_call x1, Pallas kernels: 127 us -> 125 us  [fused(): pl.pallas_call(functools.partial(fused_kernel, n), out_shape=(jax.ShapeDt...]
where the time goes in v3:
time: 132 us; the launch traced here: 131 us
  Pallas kernels  125 us (95%)
  local copies, waits for them, and re-layouts  5.34 us (4%)
    pallas_call x1, Pallas kernels, fused(): pl.pallas_call(functools.partial(fused_kernel, n), out_shape=(jax.ShapeDt...  125 us
    unnamed x12, local copies, waits for them, and re-layouts  5.13 us

profile of v3, /device:TPU:1, one launch (start us, length us, event | category | flops | bytes accessed | tf_op | source)
XLA Modules:
  0.0 131.4 jit_solution(13847416388465672065)
XLA Ops:
  0.6 0.0 copy-start.4
  0.6 0.0 copy-start.3
  0.7 0.7 copy-done.4
  1.3 0.1 constant_dynamic-slice_fusion
  1.4 0.1 reshape.8.own_ref
  1.6 0.0 copy-done.3
  1.6 0.0 copy-start
  1.6 1.2 copy-done
  2.8 0.0 copy-start.1
  2.8 1.0 copy-done.1
  3.8 0.0 copy-start.2
  3.8 0.9 copy-done.2
  4.7 125.3 %shard_map.68 = (f32[147,128]{1,0:T(8,128)S(1)}, f32[2,64,147]{2,1,0:T(8,128)S(1)}) custom-call(bf16[440,512]{1,0:T(8,128)(2,1)S(1)} %bitcast.5, f32[147,128]{1,0:T(8,128)S(1)} %bitcast.6, f32[2,64,147]{2,1,0:T(8,128)S(1)} %copy-done.2, f32[2,64,2048]{2,1,0:T(8,128)S(1)} %bitcast.4, s32[128,1]{1,0:T(8,128)S(1)} %reshape.8.own_ref, s32[2,2048]{1,0:T(2,128)S(1)} %copy-done.4), custom_call_target="tpu_custom_call" | custom-call | tf_op jit(solution)/shard_map/pallas_call | solution.py:332
  130.1 0.6 copy.10
  130.7 0.7 copy.11
Async XLA Ops:
  0.6 0.7 copy-start.4
  0.6 0.9 copy-start.3
  1.6 1.2 copy-start
  2.8 1.0 copy-start.1
  3.8 0.9 copy-start.2

commit v4 on v3

--- a/solution.py
+++ b/solution.py
@@ -272,13 +272,21 @@
         at = pl.ds(c * tile, tile)
         wanted = cols_ref[s : s + 1, at]
 
+        lines = lax.broadcasted_iota(jnp.int32, (256, tile), 0).astype(F32).astype(BF16)
+        one, zero = jnp.ones((256, tile), BF16), jnp.zeros((256, tile), BF16)
+
         def inner(f, acc):
-            frames = lax.broadcasted_iota(jnp.int32, (shard, tile), 0)
-            hot = jnp.where(frames == wanted - f * shard, 1.0, 0.0).astype(BF16)
-            here = pl.ds(pl.multiple_of(f * shard, shard), shard)
+            hots = []
+            for part in range(2 * shard // 256):
+                local = wanted - (f * 2 * shard + part * 256)
+                local = jnp.where((local >= 0) & (local < 256), local, -1)
+                local = jnp.broadcast_to(local.astype(F32).astype(BF16), (256, tile))
+                hots.append(jnp.where(lines == local, one, zero))
+            hot = jnp.concatenate(hots, axis=0)
+            here = pl.ds(pl.multiple_of(f * 2 * shard, 2 * shard), 2 * shard)
             return acc + nn_dot(kern[2 * own : 2 * own + rows, here], hot)
 
-        kcol[s, :, at] = lax.fori_loop(0, n, inner, jnp.zeros((rows, tile), F32)).astype(BF16)
+        kcol[s, :, at] = lax.fori_loop(0, n // 2, inner, jnp.zeros((rows, tile), F32)).astype(BF16)
 
     def gather(which, early=None, late=None):
         begin(which)

time: 132 us -> 132 us (level)
  no operation moved by 1% of the time
where the time goes in v4:
time: 132 us; the launch traced here: 131 us
  Pallas kernels  125 us (95%)
  local copies, waits for them, and re-layouts  5.34 us (4%)
    pallas_call x1, Pallas kernels, fused(): pl.pallas_call(functools.partial(fused_kernel, n), out_shape=(jax.ShapeDt...  125 us
    unnamed x12, local copies, waits for them, and re-layouts  5.13 us

profile of v4, /device:TPU:1, one launch (start us, length us, event | category | flops | bytes accessed | tf_op | source)
XLA Modules:
  0.0 131.4 jit_solution(7965591583382365798)
XLA Ops:
  0.6 0.0 copy-start.4
  0.6 0.0 copy-start.3
  0.7 0.7 copy-done.4
  1.3 0.1 constant_dynamic-slice_fusion
  1.4 0.1 reshape.8.own_ref
  1.6 0.0 copy-done.3
  1.6 0.0 copy-start
  1.6 1.2 copy-done
  2.8 0.0 copy-start.1
  2.8 1.0 copy-done.1
  3.8 0.0 copy-start.2
  3.8 0.9 copy-done.2
  4.7 125.3 %shard_map.68 = (f32[147,128]{1,0:T(8,128)S(1)}, f32[2,64,147]{2,1,0:T(8,128)S(1)}) custom-call(bf16[440,512]{1,0:T(8,128)(2,1)S(1)} %bitcast.5, f32[147,128]{1,0:T(8,128)S(1)} %bitcast.6, f32[2,64,147]{2,1,0:T(8,128)S(1)} %copy-done.2, f32[2,64,2048]{2,1,0:T(8,128)S(1)} %bitcast.4, s32[128,1]{1,0:T(8,128)S(1)} %reshape.8.own_ref, s32[2,2048]{1,0:T(2,128)S(1)} %copy-done.4), custom_call_target="tpu_custom_call" | custom-call | tf_op jit(solution)/shard_map/pallas_call | solution.py:340
  130.1 0.6 copy.10
  130.7 0.7 copy.11
Async XLA Ops:
  0.6 0.7 copy-start.4
  0.6 0.9 copy-start.3
  1.6 1.2 copy-start
  2.8 1.0 copy-start.1
  3.8 0.9 copy-start.2
